TPU v7x, 256 devices: a whole 4x4x8 slice. The times are simulated.
256 devices in a mesh: rep: 2 (over z_hi), ctx: 128 (over x, y, z_lo, core).
Axes of the slice: x: 4, y: 4, z: 8 (z_hi: 2, z_lo: 4; z = z_hi * 4 + z_lo), core: 2. Of those that a mesh axis runs over, the one named last changes fastest.
Arguments:
- inputs: bfloat16 [2, 16384, 4096], P('rep', 'ctx'), may hold values from -6 to 6
- gate_li: bfloat16 [2, 16384, 4096], P('rep', 'ctx'), may hold values from -6 to 6
- gate_mr: bfloat16 [2, 16384, 4096], P('rep', 'ctx'), may hold values from -6 to 6
- cotangent: bfloat16 [2, 16384, 4096], P('rep', 'ctx'), may hold values from -6 to 6
- residues: float32 [128, 16], replicated, may hold values from -1.5 to 1.5
- rates: float32 [128, 16], replicated, may hold values from 1.2207031e-05 to 0.05
- taps: float32 [128, 128], replicated, may hold values from -0.5 to 0.5
Outputs:
- grad_inputs: bfloat16 [2, 16384, 4096], P('rep', 'ctx')
- grad_gate_li: bfloat16 [2, 16384, 4096], P('rep', 'ctx')
- grad_gate_mr: bfloat16 [2, 16384, 4096], P('rep', 'ctx')
- grad_residues: float32 [128, 16], replicated
- grad_taps: float32 [128, 128], replicated
All inputs are finite; a program needn't handle non-finite values.
Results may differ from a plain program's by a relative error of at most 0.0049.
Values may be sent and summed in bfloat16 or wider, within the bound.
No kernel may reach another device: no remote copies, remote signals or barrier semaphores. Data moves between devices by JAX's collectives and lax.ppermute only.
A program may use at most 320 MiB of HBM per device.

v0:
```python
import math
import jax
import jax.numpy as jnp
from jax import lax
from jax.sharding import PartitionSpec as P


def from_behind(block, axis, distance):
    devices = range(lax.axis_size(axis))
    route = [(i - distance, i) for i in devices if i - distance in devices]
    return lax.ppermute(block, axis, route)


def contract(form, left_op, right_op):
    return jnp.einsum(form, left_op, right_op, precision=lax.Precision.HIGHEST)


def diagonal_matrix(diag_vals, rows, cols):
    lead = diag_vals.shape[:-1]
    period = rows + cols
    reverse_vals = jnp.flip(diag_vals, -1)
    padded = jnp.concatenate([reverse_vals, jnp.zeros(lead + (1,), reverse_vals.dtype)], axis=-1)
    tiled = jnp.tile(padded, (1,) * len(lead) + (rows + 1,))
    window = tiled[..., rows - 1 : rows - 1 + rows * (period - 1)]
    return window.reshape(lead + (rows, period - 1))[..., :cols]


def li_matrix(kernel):
    block_len = kernel.shape[-1]
    lead = kernel.shape[:-1]
    diag_vals = jnp.concatenate([jnp.zeros(lead + (block_len - 1,), kernel.dtype), kernel], axis=-1)
    return diagonal_matrix(diag_vals, block_len, block_len)


def mr_matrix(tap_rows):
    block_len = tap_rows.shape[-1]
    lead = tap_rows.shape[:-1]
    diag_vals = jnp.concatenate(
        [
            jnp.zeros(lead + (block_len - 1,), tap_rows.dtype),
            tap_rows,
            jnp.zeros(lead + (block_len,), tap_rows.dtype),
        ],
        axis=-1,
    )
    return diagonal_matrix(diag_vals, block_len, 2 * block_len)


def mode_tables(rates_part, residues_part, block_len):
    steps_up = jnp.arange(block_len).astype(jnp.float32)
    lam_rows = jnp.exp(-rates_part[:, :, None] * steps_up)
    norm_factor = jnp.sqrt(-jnp.expm1(-2.0 * rates_part))
    weight = residues_part * norm_factor
    kernel = contract("gm,gmk->gk", weight, lam_rows)
    toeplitz = li_matrix(kernel)
    end_powers = jnp.exp(-rates_part[:, :, None] * (block_len - 1.0 - steps_up))
    starts = jnp.exp(-rates_part[:, :, None] * (steps_up + 1.0))
    decay_rate = jnp.exp(-rates_part * block_len)
    return (toeplitz, lam_rows, end_powers, starts, decay_rate, norm_factor, weight, kernel)


def link_states(earlier, later_one):
    return (earlier[0] * later_one[0], later_one[0] * earlier[1] + later_one[1])


def nothing_before(total_a, total_b):
    return jnp.zeros_like(total_b)


def chain_states(decay_rate, block_ends, outside):
    nblocks = block_ends.shape[0]
    factor = jnp.broadcast_to(
        decay_rate.T[None, :, :, None], (nblocks,) + decay_rate.T.shape + (1,)
    )
    inc_a, inc_b = lax.associative_scan(link_states, (factor, block_ends), axis=0)
    before_a = jnp.concatenate([jnp.ones_like(inc_a[:1]), inc_a[:-1]], axis=0)
    before_b = jnp.concatenate([jnp.zeros_like(inc_b[:1]), inc_b[:-1]], axis=0)
    from_device = outside(inc_a[-1], inc_b[-1])
    return before_b + before_a * from_device[None]


def long_filter(seq_blocks, tables, outside):
    toeplitz, lam_rows, end_powers, starts, decay_rate, norm_factor, weight, kernel = tables
    local_part = contract("gtu,nugc->ntgc", toeplitz, seq_blocks)
    block_ends = contract("gmu,nugc->nmgc", end_powers, seq_blocks)
    entering = chain_states(decay_rate, block_ends, outside)
    carried = contract("gmt,nmgc->ntgc", starts * weight[:, :, None], entering)
    return (local_part + carried, entering)


def residue_grad(cot_blocks, seq_blocks, entering, tables):
    toeplitz, lam_rows, end_powers, starts, decay_rate, norm_factor, weight, kernel = tables
    cross_terms = contract("ntgc,nugc->gtu", cot_blocks, seq_blocks)
    unused_value, pull_back = jax.vjp(li_matrix, kernel)
    lag_totals = pull_back(cross_terms)[0]
    from_before = contract("gmt,ntgc->nmgc", starts, cot_blocks)
    first_part = jnp.sum(from_before * entering, axis=(0, 3)).T
    return norm_factor * (first_part + contract("gk,gmk->gm", lag_totals, lam_rows))


def make_pairs(extended, block_len):
    nblocks = extended.shape[0] // block_len - 1
    split_rows = extended.reshape((nblocks + 1, block_len) + extended.shape[1:])
    return jnp.concatenate([split_rows[:-1], split_rows[1:]], axis=1)


def on_device(inputs, gate_li, gate_mr, cotangent, residues, rates, taps):
    row_count = inputs.shape[1]
    width_all = inputs.shape[2]
    block_len = taps.shape[1]
    groups_all = residues.shape[0]
    group_size = width_all // groups_all
    blocks_dev = row_count // block_len
    gate_one = gate_li[0].astype(jnp.float32)
    gate_two = gate_mr[0].astype(jnp.float32)
    cot_out = cotangent[0].astype(jnp.float32)
    ctx_count = lax.axis_size("ctx")
    local_width = width_all // ctx_count
    members = min(group_size, local_width)
    owned_groups = local_width // members
    first_group = lax.axis_index("ctx") * local_width // group_size
    rates_part = lax.dynamic_slice_in_dim(rates, first_group, owned_groups, 0)
    residues_part = lax.dynamic_slice_in_dim(residues, first_group, owned_groups, 0)
    tables = mode_tables(rates_part, residues_part, block_len)
    spread = lax.all_to_all(inputs, "ctx", split_axis=2, concat_axis=1, tiled=True)
    seq_rows = spread.shape[1]
    seq_blocks = (
        spread[0]
        .astype(jnp.float32)
        .reshape(seq_rows // block_len, block_len, owned_groups, members)
    )
    values_ch, entering = long_filter(seq_blocks, tables, nothing_before)
    values = lax.all_to_all(
        values_ch.reshape(1, seq_rows, local_width), "ctx", split_axis=1, concat_axis=2, tiled=True
    )[0]
    mixer_in = (gate_one * values).astype(jnp.bfloat16)
    before = from_behind(mixer_in, "ctx", 1)
    extended = jnp.concatenate([before, mixer_in], axis=0)
    extended = extended.astype(jnp.float32).reshape(row_count + block_len, groups_all, group_size)
    in_pairs = make_pairs(extended, block_len)
    forward_taps = mr_matrix(taps)
    mixed_out = contract("gts,nsgc->ntgc", forward_taps, in_pairs).reshape(row_count, width_all)
    grad_gate_mr = (cot_out * mixed_out).astype(jnp.bfloat16)
    scaled = (cot_out * gate_two).astype(jnp.bfloat16)
    rows_after = from_behind(scaled, "ctx", -1)
    ext_cot = jnp.concatenate([scaled, rows_after], axis=0)
    ext_cot = ext_cot.astype(jnp.float32).reshape(row_count + block_len, groups_all, group_size)
    cot_pairs = jnp.flip(make_pairs(ext_cot, block_len), 1)
    grad_mixer = jnp.flip(contract("gts,nsgc->ntgc", forward_taps, cot_pairs), 1).reshape(
        row_count, width_all
    )
    scaled_blocks = scaled.astype(jnp.float32).reshape(
        blocks_dev, block_len, groups_all, group_size
    )
    cross_taps = contract("ntgc,nsgc->gts", scaled_blocks, in_pairs)
    unused_matrix, tap_pull = jax.vjp(mr_matrix, taps)
    grad_taps = tap_pull(cross_taps)[0]
    grad_gate_li = (grad_mixer * values).astype(jnp.bfloat16)
    cot_li = grad_mixer * gate_one
    cot_spread = lax.all_to_all(cot_li[None], "ctx", split_axis=2, concat_axis=1, tiled=True)[0]
    cot_blocks = cot_spread.reshape(seq_rows // block_len, block_len, owned_groups, members)
    flipped = jnp.flip(cot_blocks, (0, 1))
    back_blk, unused_states = long_filter(flipped, tables, nothing_before)
    back_ch = jnp.flip(back_blk, (0, 1)).reshape(1, seq_rows, local_width)
    grad_inputs = lax.all_to_all(
        back_ch.astype(jnp.bfloat16), "ctx", split_axis=1, concat_axis=2, tiled=True
    ).astype(back_ch.dtype)[0]
    part_res = residue_grad(cot_blocks, seq_blocks, entering, tables)
    grad_res = lax.dynamic_update_slice_in_dim(jnp.zeros_like(residues), part_res, first_group, 0)
    summed = lax.psum((grad_res, grad_taps), ("rep", "ctx"))
    grad_scale = 1.0 / math.sqrt(lax.axis_size("rep") * seq_rows)
    return (
        grad_inputs.astype(jnp.bfloat16)[None],
        grad_gate_li[None],
        grad_gate_mr[None],
        summed[0] * grad_scale,
        summed[1] * grad_scale,
    )


def solution(mesh):
    in_specs = (
        P("rep", "ctx", None),
        P("rep", "ctx", None),
        P("rep", "ctx", None),
        P("rep", "ctx", None),
        P(),
        P(),
        P(),
    )
    out_specs = (P("rep", "ctx", None), P("rep", "ctx", None), P("rep", "ctx", None), P(), P())
    return jax.shard_map(
        on_device, mesh=mesh, in_specs=in_specs, out_specs=out_specs, check_vma=False
    )
```

profile of v0, /device:TPU:1, one launch (start us, length us, event | category | flops | bytes accessed | tf_op | source)
XLA Modules:
  0.0 1296.1 jit_solution(12394947973667064074)
XLA Ops:
  7.2 5.0 copy.187
  12.7 22.3 %reduce.7 = bf16[4096,128]{1,0:T(8,128)(2,1)S(1)} reduce(bf16[4096,1,128]{2,1,0:T(2,128)(2,1)S(1)} %bitcast.245, bf16[]{:T(256)} %broadcast.484), dimensions={1}, to_apply=%bitcast.210.reduce_sub_computation | reduce | bytes 2097154
  36.2 14.1 %all-to-all-start.2 = ((bf16[128,2,2048]{2,1,0:T(2,128)(2,1)}), bf16[128,2,2048]{2,1,0:T(2,128)(2,1)S(1)}, u32[]{:S(2)}, u32[]{:S(2)}) async-start(bf16[128,2,2048]{2,1,0:T(2,128)(2,1)} %reshape.684), calls=%async_computation.2 | async-start | bytes 2097152 | tf_op jit(solution)/shard_map/all_to_all | solution.py:125
  56.7 23.0 %all-to-all-done.2 = bf16[128,2,2048]{2,1,0:T(2,128)(2,1)S(1)} async-done(((bf16[128,2,2048]{2,1,0:T(2,128)(2,1)}), bf16[128,2,2048]{2,1,0:T(2,128)(2,1)S(1)}, u32[]{:S(2)}, u32[]{:S(2)}) %all-to-all-start.2) | async-done | bytes 1048608 | tf_op jit(solution)/shard_map/all_to_all | solution.py:125
  88.0 22.4 %pad.354 = f32[128,16,1,32]{3,1,0,2:T(8,128)S(1)} pad(f32[64,16,1,32]{3,1,0,2:T(8,128)} %add.351, f32[]{:T(128)} %constant.15.clone.1), padding=1_0_1x0_0_0x0_0_0x0_0_0 | pad | bytes 393220
  118.7 13.9 %copy.193 = f32[1,16384,32]{2,0,1:T(1,128)} copy(f32[1,16384,32]{1,0,2:T(1,128)S(1)} %bitcast.242) | data formatting | bytes 4194304 | tf_op jit(solution)/shard_map/reshape | solution.py:134
  133.1 74.7 %reduce.8 = f32[16384,32]{1,0:T(8,128)} reduce(f32[16384,1,32]{2,1,0:T(1,128)} %bitcast.224, f32[]{:T(128)} %broadcast.485), dimensions={1}, to_apply=%bitcast.212.reduce_sub_computation | reduce | bytes 4194308
  207.8 7.8 reshape.686
  215.6 8.0 all-to-all-start.3
  224.3 50.9 %all-to-all-done.3 = f32[128,1,4096]{2,1,0:T(1,128)} async-done(((f32[128,1,4096]{2,1,0:T(1,128)}), f32[128,1,4096]{2,1,0:T(1,128)}, u32[]{:S(2)}, u32[]{:S(2)}) %all-to-all-start.3) | async-done | bytes 2097184 | tf_op jit(solution)/shard_map/all_to_all | solution.py:133
  275.1 7.3 reduce.9
  282.5 15.5 %reshape.687 = f32[16384,1,32]{2,1,0:T(1,128)} reshape(f32[128,4096]{1,0:T(8,128)S(1)} %reduce.9) | data formatting | bytes 4194304
  297.9 19.4 %copy.194 = f32[1,16384,32]{1,0,2:T(1,128)} copy(f32[1,16384,32]{2,0,1:T(1,128)} %bitcast.225) | data formatting | bytes 4194304 | tf_op jit(solution)/shard_map/all_to_all | solution.py:133
  324.5 11.5 tile.20
  336.0 17.0 %slice.430 = f32[128,49024]{0,1:T(8,128)} slice(f32[128,49536]{0,1:T(8,128)} %bitcast.223), slice={[0:128], [127:49151]} | slice | bytes 50200576 | tf_op jit(solution)/shard_map/slice | solution.py:24
  353.0 22.3 %reshape.679 = f32[128,128,383]{0,2,1:T(8,128)} reshape(f32[128,49024]{0,1:T(8,128)} %slice.430) | data formatting | bytes 50200576 | tf_op jit(solution)/shard_map/reshape | solution.py:25
  375.3 11.6 slice.431
  387.0 17.7 %copy.208 = f32[128,128,256]{2,1,0:T(8,128)} copy(f32[128,128,256]{0,2,1:T(8,128)} %slice.431) | data formatting | bytes 33554432
  411.3 21.5 %fusion.3 = f32[128,32,128]{2,1,0:T(8,128)S(1)} fusion(f32[128,128,256]{2,1,0:T(8,128)} %copy.208, f32[1,128,128,32]{1,3,2,0:T(8,128)S(1)} %bitcast.234, f32[1,128,128,32]{1,3,2,0:T(8,128)S(1)} %bitcast.232), kind=kOutput, calls=%fused_computation.5 | convolution fusion | flops 1611661312 | bytes 23068672 | tf_op jit(solution)/shard_map/gts,nsgc->ntgc/dot_general | solution.py:15
  437.6 12.7 collective-permute-done
  453.4 7.4 rev.27
  460.8 22.1 %fusion.12 = f32[1,128,128,32]{1,3,2,0:T(8,128)} fusion(f32[128,128,256]{2,1,0:T(8,128)} %copy.208, f32[1,256,128,32]{1,3,2,0:T(8,128)} %rev.27), kind=kOutput, calls=%fused_computation.23 | convolution fusion | flops 1610612736 | bytes 23068672 | tf_op jit(solution)/shard_map/gts,nsgc->ntgc/dot_general | solution.py:15
  482.9 4.2 rev.29
  490.2 67.2 %all_to_all.63 = f32[1,128,4096]{1,0,2:T(1,128)S(1)} all-to-all(f32[1,128,4096]{1,0,2:T(1,128)S(1)} %bitcast.246), channel_id=1, replica_groups=mesh['rep'=2,'ctx'=128] {'ctx'}, dimensions={2} | all-to-all | bytes 4194304 | tf_op jit(solution)/shard_map/all_to_all | solution.py:160
  559.7 9.8 convolution_bitcast_fusion.1
  592.8 4.7 pad.167
  600.2 8.5 pad.170
  612.2 15.1 %pad.172 = f32[64,16,1,32]{3,1,0,2:T(8,128)} pad(f32[32,16,1,32]{3,1,0,2:T(8,128)} %add.316, f32[]{:T(128)} %constant.15.clone.1), padding=1_0_1x0_0_0x0_0_0x0_0_0 | pad | bytes 196612 | tf_op jit(solution)/shard_map/pad | solution.py:75
  628.3 10.3 pad.171
  641.0 20.1 %pad.258 = f32[127,16,1,32]{3,1,0,2:T(8,128)} pad(f32[64,16,1,32]{3,1,0,2:T(8,128)S(1)} %pad_maximum_fusion.1, f32[]{:T(128)} %constant.15.clone.1), padding=0_0_1x0_0_0x0_0_0x0_0_0 | pad | bytes 391172 | tf_op jit(solution)/shard_map/slice | solution.py:77
  661.1 22.4 %pad.352 = f32[128,16,1,32]{3,1,0,2:T(8,128)S(1)} pad(f32[64,16,1,32]{3,1,0,2:T(8,128)} %add.318, f32[]{:T(128)} %constant.15.clone.1), padding=1_0_1x0_0_0x0_0_0x0_0_0 | pad | bytes 393220
  685.8 3.5 fusion.47
  692.6 11.4 rev.32
  705.5 12.8 copy.184
  718.3 91.1 %reduce.10 = bf16[16384,32]{1,0:T(8,128)(2,1)} reduce(bf16[16384,1,32]{2,1,0:T(2,128)(2,1)} %bitcast.226, bf16[]{:T(256)} %broadcast.484), dimensions={1}, to_apply=%bitcast.208.reduce_sub_computation | reduce | bytes 2097154
  809.4 7.3 reshape.682
  816.7 7.5 all-to-all-start.1
  824.3 8.8 fusion.2
  833.2 9.1 pad.205
  842.3 26.8 %reshape.667 = f32[128,49024]{1,0:T(8,128)} reshape(f32[128,128,383]{2,1,0:T(8,128)} %pad.205) | data formatting | bytes 50200576 | tf_op jit(solution)/shard_map/transpose(jvp())/reshape | solution.py:25
  869.1 24.7 %copy.212 = f32[128,49024]{0,1:T(8,128)} copy(f32[128,49024]{1,0:T(8,128)} %reshape.667) | data formatting | bytes 50200576
  893.8 19.2 %pad.206.clone = f32[128,49536]{0,1:T(8,128)} pad(f32[128,49024]{0,1:T(8,128)} %copy.212, f32[]{:T(128)} %constant.15.clone.1), padding=0_0x127_385 | pad | bytes 50462724 | tf_op jit(solution)/shard_map/transpose(jvp())/pad | solution.py:24
  913.0 9.3 reduce_sum.32
  925.3 236.1 %all-reduce.53.cloned.1.call-done = f32[128,128]{0,1:T(8,128)} async-done(((f32[128,128]{0,1:T(8,128)}), f32[128,128]{0,1:T(8,128)}) %all-reduce.53.cloned.1.call-update) | async-done | bytes 65552 | tf_op jit(solution)/shard_map/psum | solution.py:170
  1168.3 9.6 fusion.18
  1178.3 74.4 %psum.14 = f32[128,16]{0,1:T(8,128)S(1)} all-reduce(f32[128,16]{0,1:T(8,128)S(1)} %dynamic_update_slice.3), channel_id=1, replica_groups=mesh['rep'=2,'ctx'=128] {'rep','ctx'}, use_global_device_ids=true, to_apply=%region_2.3 | all-reduce | flops 2048 | bytes 16384 | tf_op jit(solution)/shard_map/psum | solution.py:170
  1253.3 18.4 %reshape.683 = bf16[16384,1,32]{2,1,0:T(2,128)(2,1)} reshape(bf16[128,2,2048]{2,1,0:T(2,128)(2,1)} %all-to-all-done.1) | data formatting | bytes 2097152
  1271.7 15.1 %copy.185 = bf16[1,16384,32]{1,2,0:T(8,128)(2,1)S(1)} copy(bf16[1,16384,32]{2,0,1:T(2,128)(2,1)} %bitcast.227) | data formatting | bytes 2097152 | tf_op jit(solution)/shard_map/all_to_all | solution.py:165
  (289 shorter events, 105.1 us)
Async XLA Ops:
  35.0 15.3 %copy-start.32 = (f32[128,16]{0,1:T(8,128)S(1)}, f32[128,16]{0,1:T(8,128)}, u32[]{:S(2)}) copy-start(f32[128,16]{0,1:T(8,128)} %param.12) | copy-start | bytes 24580
  35.0 15.3 %copy-start.33 = (f32[128,16]{0,1:T(8,128)S(1)}, f32[128,16]{0,1:T(8,128)}, u32[]{:S(2)}) copy-start(f32[128,16]{0,1:T(8,128)} %param.11) | copy-start | bytes 24580
  36.2 43.5 %all-to-all-start.2 = ((bf16[128,2,2048]{2,1,0:T(2,128)(2,1)}), bf16[128,2,2048]{2,1,0:T(2,128)(2,1)S(1)}, u32[]{:S(2)}, u32[]{:S(2)}) async-start(bf16[128,2,2048]{2,1,0:T(2,128)(2,1)} %reshape.684), calls=%async_computation.2 | async-start | bytes 2097152 | tf_op jit(solution)/shard_map/all_to_all | solution.py:125
  50.5 4.1 copy-start.42
  50.5 519.0 %copy-start.20 = (f32[1,16]{1,0:T(1,128)}, f32[1,16]{1,0:T(1,128)S(1)}, u32[]{:S(2)}) copy-start(f32[1,16]{1,0:T(1,128)S(1)} %get-tuple-element.31) | copy-start | bytes 196
  50.5 32.5 %copy-start.36 = (f32[16]{0:T(128)}, f32[16]{0:T(128)S(1)}, u32[]{:S(2)}) copy-start(f32[16]{0:T(128)S(1)} %get-tuple-element.57) | copy-start | bytes 196
  50.5 32.6 %copy-start.30 = (f32[16]{0:T(128)}, f32[16]{0:T(128)S(1)}, u32[]{:S(2)}) copy-start(f32[16]{0:T(128)S(1)} %get-tuple-element.60) | copy-start | bytes 196
  50.5 32.7 %copy-start.28 = (f32[16]{0:T(128)}, f32[16]{0:T(128)S(1)}, u32[]{:S(2)}) copy-start(f32[16]{0:T(128)S(1)} %get-tuple-element.59) | copy-start | bytes 196
  50.6 32.9 %copy-start.26 = (f32[16]{0:T(128)}, f32[16]{0:T(128)S(1)}, u32[]{:S(2)}) copy-start(f32[16]{0:T(128)S(1)} %get-tuple-element.58) | copy-start | bytes 196
  50.6 519.1 %copy-start.22 = (f32[16]{0:T(128)}, f32[16]{0:T(128)S(1)}, u32[]{:S(2)}) copy-start(f32[16]{0:T(128)S(1)} %get-tuple-element.62) | copy-start | bytes 196
  50.6 520.0 %copy-start.25 = (f32[16]{0:T(128)}, f32[16]{0:T(128)S(1)}, u32[]{:S(2)}) copy-start(f32[16]{0:T(128)S(1)} %get-tuple-element.61) | copy-start | bytes 196
  54.3 26.5 %copy-start.44 = (f32[128]{0:T(128)}, f32[128]{0:T(128)S(1)}, u32[]{:S(2)}) copy-start(f32[128]{0:T(128)S(1)} %iota_convert_fusion) | copy-start | bytes 1540
  54.3 58.1 %copy-start.38 = (f32[16]{0:T(128)}, f32[16]{0:T(128)S(1)}, u32[]{:S(2)}) copy-start(f32[16]{0:T(128)S(1)} %get-tuple-element.48) | copy-start | bytes 196
  54.3 505.4 %copy-start.23 = (f32[16]{0:T(128)}, f32[16]{0:T(128)S(1)}, u32[]{:S(2)}) copy-start(f32[16]{0:T(128)S(1)} %get-tuple-element.49) | copy-start | bytes 196
  56.5 24.4 %copy-start.40 = (f32[128]{0:T(128)}, f32[128]{0:T(128)S(1)}, u32[]{:S(2)}) copy-start(f32[128]{0:T(128)S(1)} %broadcast_subtract_fusion) | copy-start | bytes 1540
  56.5 55.9 %copy-start.34 = (f32[128]{0:T(128)}, f32[128]{0:T(128)S(1)}, u32[]{:S(2)}) copy-start(f32[128]{0:T(128)S(1)} %broadcast_add_fusion) | copy-start | bytes 1540
  56.7 53.9 %copy-start.13 = (f32[128,16,1,1]{1,3,2,0:T(1,128)}, f32[128,16,1,1]{1,3,2,0:T(1,128)S(1)}, u32[]{:S(2)}) copy-start(f32[128,16,1,1]{1,3,2,0:T(1,128)S(1)} %pad_multiply_fusion) | copy-start | bytes 24580
  80.9 33.4 %copy-start.3 = (bf16[1,128,4096]{1,2,0:T(8,128)(2,1)}, bf16[1,128,4096]{1,2,0:T(8,128)(2,1)S(1)}, u32[]{:S(2)}) copy-start(bf16[1,128,4096]{1,2,0:T(8,128)(2,1)S(1)} %copy.207) | copy-start | bytes 3145732
  110.6 1.0 copy-start.7
  111.9 2.4 copy-start.16
  215.6 8.0 copy-start.15
  215.6 59.5 %all-to-all-start.3 = ((f32[128,1,4096]{2,1,0:T(1,128)}), f32[128,1,4096]{2,1,0:T(1,128)}, u32[]{:S(2)}, u32[]{:S(2)}) async-start(f32[128,1,4096]{2,1,0:T(1,128)} %reshape.686), calls=%async_computation.3 | async-start | bytes 4194304 | tf_op jit(solution)/shard_map/all_to_all | solution.py:133
  320.2 3.2 copy-start.19
  321.4 87.8 %collective-permute-start.1 = (bf16[128,4096]{0,1:T(8,128)(2,1)}, bf16[128,4096]{0,1:T(8,128)(2,1)}, u32[]{:S(2)}, u32[]{:S(2)}) collective-permute-start(bf16[128,4096]{0,1:T(8,128)(2,1)} %fusion.7), channel_id=1, source_target_pairs={{0,1},{1,2},{2,3},{3,4},{4,5},{5,6},{6,7},{7,8},{8,9},{9,10},{10,1... | collective-permute-start | bytes 3145736 | tf_op jit(solution)/shard_map/ppermute | solution.py:11
  411.3 21.5 %copy-start.1 = (f32[128,4096]{0,1:T(8,128)}, f32[128,4096]{0,1:T(8,128)S(1)}, u32[]{:S(2)}) copy-start(f32[128,4096]{0,1:T(8,128)S(1)} %get-tuple-element.32) | copy-start | bytes 6291460
  411.3 21.5 %copy-start.2 = (f32[128,4096]{0,1:T(8,128)}, f32[128,4096]{0,1:T(8,128)S(1)}, u32[]{:S(2)}) copy-start(f32[128,4096]{0,1:T(8,128)S(1)} %get-tuple-element.33) | copy-start | bytes 6291460
  411.3 21.5 %copy-start.10 = (bf16[1,128,4096]{1,2,0:T(8,128)(2,1)S(1)}, bf16[1,128,4096]{1,2,0:T(8,128)(2,1)}, u32[]{:S(2)}) copy-start(bf16[1,128,4096]{1,2,0:T(8,128)(2,1)} %copy.174) | copy-start | bytes 3145732
  411.3 21.5 %copy-start.11 = (bf16[1,128,4096]{1,2,0:T(8,128)(2,1)S(1)}, bf16[1,128,4096]{1,2,0:T(8,128)(2,1)}, u32[]{:S(2)}) copy-start(bf16[1,128,4096]{1,2,0:T(8,128)(2,1)} %copy.175) | copy-start | bytes 3145732
  434.2 16.1 %copy-start.5 = (bf16[1,128,4096]{1,2,0:T(8,128)(2,1)}, bf16[1,128,4096]{1,2,0:T(8,128)(2,1)S(1)}, u32[]{:S(2)}) copy-start(bf16[1,128,4096]{1,2,0:T(8,128)(2,1)S(1)} %get-tuple-element.39) | copy-start | bytes 3145732
  434.2 16.1 %collective-permute-start = (bf16[128,4096]{0,1:T(8,128)(2,1)S(1)}, bf16[128,4096]{0,1:T(8,128)(2,1)S(1)}, u32[]{:S(2)}, u32[]{:S(2)}) collective-permute-start(bf16[128,4096]{0,1:T(8,128)(2,1)S(1)} %bitcast.239), channel_id=1, source_target_pairs={{1,0},{2,1},{3,2},{4,3},{5,4},{6,5},{7,6},{8,7},{9,8},{10,9},{11,1... | collective-permute-start | bytes 3145736 | tf_op jit(solution)/shard_map/ppermute | solution.py:11
  557.3 2.4 copy-start.41
  569.5 1.2 copy-start.27
  569.5 1.2 copy-start.29
  569.5 1.3 copy-start.31
  569.6 1.4 copy-start.37
  598.4 28.9 %slice-start = ((f32[64,16,1,32]{3,1,0,2:T(8,128)}), f32[1,16,1,32]{3,1,0,2:T(8,128)S(1)}, s32[]{:S(2)}) async-start(f32[64,16,1,32]{3,1,0,2:T(8,128)} %copy-done.12), calls=%async_computation.5 | async-start | bytes 16384 | tf_op jit(solution)/shard_map/slice | solution.py:75
  600.1 38.5 %copy-start.21 = (f32[1,16]{1,0:T(1,128)S(1)}, f32[1,16]{1,0:T(1,128)}, u32[]{:S(2)}) copy-start(f32[1,16]{1,0:T(1,128)} %copy-done.20) | copy-start | bytes 196
  638.6 1.4 copy-start.8
  638.6 1.5 copy-start.9
  661.1 23.7 %copy-start.14 = (f32[128,16,1,1]{1,3,2,0:T(1,128)S(1)}, f32[128,16,1,1]{1,3,2,0:T(1,128)}, u32[]{:S(2)}) copy-start(f32[128,16,1,1]{1,3,2,0:T(1,128)} %copy-done.13) | copy-start | bytes 24580
  685.7 3.5 copy-start
  685.7 3.5 copy-start.17
  816.7 7.6 copy-start.6
  816.7 436.6 %all-to-all-start.1 = ((bf16[128,2,2048]{2,1,0:T(2,128)(2,1)}), bf16[128,2,2048]{2,1,0:T(2,128)(2,1)}, u32[]{:S(2)}, u32[]{:S(2)}) async-start(bf16[128,2,2048]{2,1,0:T(2,128)(2,1)} %reshape.682), calls=%async_computation.1 | async-start | bytes 2097152 | tf_op jit(solution)/shard_map/all_to_all | solution.py:165
  824.2 337.1 %all-reduce.53.cloned.1.call-start = ((), (), s32[]{:S(2)}) async-start(), calls=%async_computation.4 | async-start | bytes 131072 | tf_op jit(solution)/shard_map/psum | solution.py:170
  922.9 242.5 %copy-start.4 = (bf16[1,128,4096]{1,2,0:T(8,128)(2,1)S(1)}, bf16[1,128,4096]{1,2,0:T(8,128)(2,1)}, u32[]{:S(2)}) copy-start(bf16[1,128,4096]{1,2,0:T(8,128)(2,1)} %copy-done.3) | copy-start | bytes 3145732
  1167.3 10.6 copy-start.43
  1167.3 10.6 copy-start.45
  (5 other events, 4.3 us)
Sparse Core Ops, SparseCore 0:
  923.1 238.2 all-reduce.52
where the time goes:
time: 1310 us; the launch traced here: 1300 us
  local copies, waits for them, and re-layouts  453 us (35%)
  waiting for transfers between devices  323 us (25%)
  other arithmetic  243 us (19%)
  blocking collectives  142 us (11%)
  matrix products  86.1 us (7%)
  starting transfers between devices  35 us (3%)
  between operations  15.5 us (1%)
    psum x1, waiting for transfers between devices, on_device(): summed = lax.psum((grad_res, grad_taps), ('rep', 'ctx'))  236 us
    unnamed x3, other arithmetic  188 us
    unnamed x124, local copies, waits for them, and re-layouts  161 us
    dot_general x13, matrix products, contract(): return jnp.einsum(form, left_op, right_op, precision=lax.Precision.HIGHEST)  86.1 us
    psum x1, blocking collectives, on_device(): summed = lax.psum((grad_res, grad_taps), ('rep', 'ctx'))  74.4 us
    all_to_all x1, blocking collectives, on_device(): lax.all_to_all(cot_li[None], 'ctx', split_axis=2, concat_axis=1, tiled=True)  67.2 us
    pad x30, local copies, waits for them, and re-layouts, chain_states(): lax.associative_scan(link_states, (factor, block_ends), axis=0)  53 us
    all_to_all x1, waiting for transfers between devices, on_device(): lax.all_to_all(values_ch.reshape(1, seq_rows, local_width), 'ctx', split_...  50.9 us
  transfers between devices with their start and end apart: 6, of which 4 were waited for; matrix products, arithmetic and copies ran while one was open for 16% of the time, Pallas kernels for 0%

commit v1 on v0

--- a/solution.py
+++ b/solution.py
@@ -130,8 +130,16 @@
         .reshape(seq_rows // block_len, block_len, owned_groups, members)
     )
     values_ch, entering = long_filter(seq_blocks, tables, nothing_before)
-    values = lax.all_to_all(
-        values_ch.reshape(1, seq_rows, local_width), "ctx", split_axis=1, concat_axis=2, tiled=True
+    values = jnp.concatenate(
+        lax.all_to_all(
+            jnp.stack(
+                jnp.split(values_ch.reshape(1, seq_rows, local_width), lax.axis_size("ctx"), axis=1)
+            ),
+            "ctx",
+            0,
+            0,
+        ),
+        axis=2,
     )[0]
     mixer_in = (gate_one * values).astype(jnp.bfloat16)
     before = from_behind(mixer_in, "ctx", 1)

time: 1310 us -> 1250 us (0.954)
  other arithmetic: 243 us -> 160 us
  local copies, waits for them, and re-layouts: 453 us -> 472 us
    unnamed x3 -> x2, other arithmetic: 188 us -> 113 us
    unnamed x124 -> x246, local copies, waits for them, and re-layouts: 161 us -> 214 us
    all_to_all x2 -> x0, local copies, waits for them, and re-layouts: 22.2 us -> none  [on_device(): lax.all_to_all(values_ch.reshape(1, seq_rows, local_width), 'ctx', split_...]
    reshape x1 -> x0, local copies, waits for them, and re-layouts: 13.9 us -> none  [on_device(): values_ch.reshape(1, seq_rows, local_width)]
  transfers between devices with their start and end apart: 6 -> 6, of which waited for: 4 -> 4; matrix products, arithmetic and copies ran while one was open for 16% -> 17% of each run, Pallas kernels for 0% -> 0%
where the time goes in v1:
time: 1250 us; the launch traced here: 1230 us
  local copies, waits for them, and re-layouts  472 us (38%)
  waiting for transfers between devices  322 us (26%)
  other arithmetic  160 us (13%)
  blocking collectives  142 us (11%)
  matrix products  86.1 us (7%)
  starting transfers between devices  34.2 us (3%)
  between operations  15.7 us (1%)
    psum x1, waiting for transfers between devices, on_device(): summed = lax.psum((grad_res, grad_taps), ('rep', 'ctx'))  236 us
    unnamed x246, local copies, waits for them, and re-layouts  214 us
    unnamed x2, other arithmetic  113 us
    dot_general x13, matrix products, contract(): return jnp.einsum(form, left_op, right_op, precision=lax.Precision.HIGHEST)  86.1 us
    psum x1, blocking collectives, on_device(): summed = lax.psum((grad_res, grad_taps), ('rep', 'ctx'))  74.4 us
    all_to_all x1, blocking collectives, on_device(): lax.all_to_all(cot_li[None], 'ctx', split_axis=2, concat_axis=1, tiled=True)  67.4 us
    pad x30, local copies, waits for them, and re-layouts, chain_states(): lax.associative_scan(link_states, (factor, block_ends), axis=0)  53 us
    reshape x4, local copies, waits for them, and re-layouts, diagonal_matrix(): return window.reshape(lead + (rows, period - 1))[..., :cols]  50.5 us
  transfers between devices with their start and end apart: 6, of which 4 were waited for; matrix products, arithmetic and copies ran while one was open for 17% of the time, Pallas kernels for 0%

profile of v1, /device:TPU:1, one launch (start us, length us, event | category | flops | bytes accessed | tf_op | source)
XLA Modules:
  0.0 1232.0 jit_solution(933222317158744882)
XLA Ops:
  7.2 5.0 copy.636
  12.7 22.3 %reduce.7 = bf16[4096,128]{1,0:T(8,128)(2,1)S(1)} reduce(bf16[4096,1,128]{2,1,0:T(2,128)(2,1)S(1)} %bitcast.628, bf16[]{:T(256)} %broadcast.484), dimensions={1}, to_apply=%bitcast.591.reduce_sub_computation | reduce | bytes 2097154
  36.2 14.5 %all-to-all-start.2 = ((bf16[128,2,2048]{2,1,0:T(2,128)(2,1)}), bf16[128,2,2048]{2,1,0:T(2,128)(2,1)S(1)}, u32[]{:S(2)}, u32[]{:S(2)}) async-start(bf16[128,2,2048]{2,1,0:T(2,128)(2,1)} %reshape.687), calls=%async_computation.2 | async-start | bytes 2097152 | tf_op jit(solution)/shard_map/all_to_all | solution.py:125
  57.0 23.0 %all-to-all-done.2 = bf16[128,2,2048]{2,1,0:T(2,128)(2,1)S(1)} async-done(((bf16[128,2,2048]{2,1,0:T(2,128)(2,1)}), bf16[128,2,2048]{2,1,0:T(2,128)(2,1)S(1)}, u32[]{:S(2)}, u32[]{:S(2)}) %all-to-all-start.2) | async-done | bytes 1048608 | tf_op jit(solution)/shard_map/all_to_all | solution.py:125
  88.4 22.4 %pad.354 = f32[128,16,1,32]{3,1,0,2:T(8,128)S(1)} pad(f32[64,16,1,32]{3,1,0,2:T(8,128)} %add.351, f32[]{:T(128)} %constant.15.clone.1), padding=1_0_1x0_0_0x0_0_0x0_0_0 | pad | bytes 393220
  198.1 6.6 all-to-all-start.3
  206.4 50.4 %all-to-all-done.3 = f32[128,1,128,32]{2,3,1,0:T(8,128)S(1)} async-done(((f32[128,1,128,32]{2,3,1,0:T(8,128)}), f32[128,1,128,32]{2,3,1,0:T(8,128)S(1)}, u32[]{:S(2)}, u32[]{:S(2)}) %all-to-all-start.3) | async-done | bytes 2097184 | tf_op jit(solution)/shard_map/all_to_all | solution.py:134
  260.7 11.5 tile.20
  272.2 17.0 %slice.430 = f32[128,49024]{0,1:T(8,128)} slice(f32[128,49536]{0,1:T(8,128)} %bitcast.602), slice={[0:128], [127:49151]} | slice | bytes 50200576 | tf_op jit(solution)/shard_map/slice | solution.py:24
  289.2 22.3 %reshape.682 = f32[128,128,383]{0,2,1:T(8,128)} reshape(f32[128,49024]{0,1:T(8,128)} %slice.430) | data formatting | bytes 50200576 | tf_op jit(solution)/shard_map/reshape | solution.py:25
  311.5 11.6 slice.431
  323.1 17.7 %copy.780 = f32[128,128,256]{2,1,0:T(8,128)} copy(f32[128,128,256]{0,2,1:T(8,128)} %slice.431) | data formatting | bytes 33554432
  347.5 21.5 %fusion.3 = f32[128,32,128]{2,1,0:T(8,128)S(1)} fusion(f32[128,128,256]{2,1,0:T(8,128)} %copy.780, f32[1,128,128,32]{1,3,2,0:T(8,128)S(1)} %bitcast.612, f32[1,128,128,32]{1,3,2,0:T(8,128)S(1)} %bitcast.610), kind=kOutput, calls=%fused_computation.5 | convolution fusion | flops 1611661312 | bytes 23068672 | tf_op jit(solution)/shard_map/gts,nsgc->ntgc/dot_general | solution.py:15
  370.4 3.6 collective-permute-start
  374.0 12.5 %collective-permute-done = bf16[128,4096]{0,1:T(8,128)(2,1)S(1)} collective-permute-done((bf16[128,4096]{0,1:T(8,128)(2,1)S(1)}, bf16[128,4096]{0,1:T(8,128)(2,1)S(1)}, u32[]{:S(2)}, u32[]{:S(2)}) %collective-permute-start) | collective-permute-done | bytes 1048608 | tf_op jit(solution)/shard_map/ppermute | solution.py:11
  389.5 7.3 rev.27
  396.8 22.1 %fusion.12 = f32[1,128,128,32]{1,3,2,0:T(8,128)} fusion(f32[128,128,256]{2,1,0:T(8,128)} %copy.780, f32[1,256,128,32]{1,3,2,0:T(8,128)} %rev.27), kind=kOutput, calls=%fused_computation.23 | convolution fusion | flops 1610612736 | bytes 23068672 | tf_op jit(solution)/shard_map/gts,nsgc->ntgc/dot_general | solution.py:15
  418.8 4.2 rev.29
  423.0 2.9 fusion.9
  425.9 67.4 %all_to_all.53 = f32[1,128,4096]{1,0,2:T(1,128)S(1)} all-to-all(f32[1,128,4096]{1,0,2:T(1,128)S(1)} %bitcast.629), channel_id=1, replica_groups=mesh['rep'=2,'ctx'=128] {'ctx'}, dimensions={2} | all-to-all | bytes 4194304 | tf_op jit(solution)/shard_map/all_to_all | solution.py:168
  495.6 9.8 convolution_bitcast_fusion.1
  514.9 3.2 pad.165
  518.2 3.2 pad.166
  524.4 2.8 pad.168
  528.7 4.7 pad.167
  536.1 8.5 pad.170
  548.2 15.1 %pad.172 = f32[64,16,1,32]{3,1,0,2:T(8,128)} pad(f32[32,16,1,32]{3,1,0,2:T(8,128)} %add.316, f32[]{:T(128)} %constant.15.clone.1), padding=1_0_1x0_0_0x0_0_0x0_0_0 | pad | bytes 196612 | tf_op jit(solution)/shard_map/pad | solution.py:75
  564.3 10.3 pad.171
  577.0 20.1 %pad.258 = f32[127,16,1,32]{3,1,0,2:T(8,128)} pad(f32[64,16,1,32]{3,1,0,2:T(8,128)S(1)} %pad_maximum_fusion.1, f32[]{:T(128)} %constant.15.clone.1), padding=0_0_1x0_0_0x0_0_0x0_0_0 | pad | bytes 391172 | tf_op jit(solution)/shard_map/slice | solution.py:77
  597.1 22.4 %pad.352 = f32[128,16,1,32]{3,1,0,2:T(8,128)S(1)} pad(f32[64,16,1,32]{3,1,0,2:T(8,128)} %add.318, f32[]{:T(128)} %constant.15.clone.1), padding=1_0_1x0_0_0x0_0_0x0_0_0 | pad | bytes 393220
  621.7 3.5 fusion.47
  625.2 3.3 add_bitcast_fusion
  628.5 11.4 rev.32
  641.4 12.8 %copy.633 = bf16[1,16384,32]{2,0,1:T(2,128)(2,1)} copy(bf16[1,16384,32]{1,2,0:T(8,128)(2,1)S(1)} %convert_element_type.106) | data formatting | bytes 2097152 | tf_op jit(solution)/shard_map/convert_element_type | solution.py:174
  654.2 90.9 %reduce.8 = bf16[16384,32]{1,0:T(8,128)(2,1)} reduce(bf16[16384,1,32]{2,1,0:T(2,128)(2,1)} %bitcast.603, bf16[]{:T(256)} %broadcast.484), dimensions={1}, to_apply=%bitcast.589.reduce_sub_computation | reduce | bytes 2097154
  745.1 7.3 reshape.685
  752.5 7.5 all-to-all-start.1
  760.1 8.9 fusion.2
  769.0 9.1 pad.205
  778.1 26.8 %reshape.670 = f32[128,49024]{1,0:T(8,128)} reshape(f32[128,128,383]{2,1,0:T(8,128)} %pad.205) | data formatting | bytes 50200576 | tf_op jit(solution)/shard_map/transpose(jvp())/reshape | solution.py:25
  804.9 24.7 %copy.911 = f32[128,49024]{0,1:T(8,128)} copy(f32[128,49024]{1,0:T(8,128)} %reshape.670) | data formatting | bytes 50200576
  829.6 19.2 %pad.206.clone = f32[128,49536]{0,1:T(8,128)} pad(f32[128,49024]{0,1:T(8,128)} %copy.911, f32[]{:T(128)} %constant.15.clone.1), padding=0_0x127_385 | pad | bytes 50462724 | tf_op jit(solution)/shard_map/transpose(jvp())/pad | solution.py:24
  848.7 9.3 reduce_sum.32
  861.0 236.1 %all-reduce.53.cloned.1.call-done = f32[128,128]{0,1:T(8,128)} async-done(((f32[128,128]{0,1:T(8,128)}), f32[128,128]{0,1:T(8,128)}) %all-reduce.53.cloned.1.call-update) | async-done | bytes 65552 | tf_op jit(solution)/shard_map/psum | solution.py:178
  1104.1 9.6 fusion.18
  1114.1 74.4 %psum.14 = f32[128,16]{0,1:T(8,128)S(1)} all-reduce(f32[128,16]{0,1:T(8,128)S(1)} %dynamic_update_slice.3), channel_id=1, replica_groups=mesh['rep'=2,'ctx'=128] {'rep','ctx'}, use_global_device_ids=true, to_apply=%region_2.3 | all-reduce | flops 2048 | bytes 16384 | tf_op jit(solution)/shard_map/psum | solution.py:178
  1189.1 18.4 %reshape.686 = bf16[16384,1,32]{2,1,0:T(2,128)(2,1)} reshape(bf16[128,2,2048]{2,1,0:T(2,128)(2,1)} %all-to-all-done.1) | data formatting | bytes 2097152
  1207.5 15.1 %copy.634 = bf16[1,16384,32]{1,2,0:T(8,128)(2,1)S(1)} copy(bf16[1,16384,32]{2,0,1:T(2,128)(2,1)} %bitcast.604) | data formatting | bytes 2097152 | tf_op jit(solution)/shard_map/all_to_all | solution.py:173
  (414 shorter events, 162.3 us)
Async XLA Ops:
  35.0 15.6 %copy-start.31 = (f32[128,16]{0,1:T(8,128)S(1)}, f32[128,16]{0,1:T(8,128)}, u32[]{:S(2)}) copy-start(f32[128,16]{0,1:T(8,128)} %param.12) | copy-start | bytes 24580
  35.0 15.6 %copy-start.32 = (f32[128,16]{0,1:T(8,128)S(1)}, f32[128,16]{0,1:T(8,128)}, u32[]{:S(2)}) copy-start(f32[128,16]{0,1:T(8,128)} %param.11) | copy-start | bytes 24580
  36.2 43.9 %all-to-all-start.2 = ((bf16[128,2,2048]{2,1,0:T(2,128)(2,1)}), bf16[128,2,2048]{2,1,0:T(2,128)(2,1)S(1)}, u32[]{:S(2)}, u32[]{:S(2)}) async-start(bf16[128,2,2048]{2,1,0:T(2,128)(2,1)} %reshape.687), calls=%async_computation.2 | async-start | bytes 2097152 | tf_op jit(solution)/shard_map/all_to_all | solution.py:125
  50.8 4.1 copy-start.41
  50.8 454.6 %copy-start.19 = (f32[1,16]{1,0:T(1,128)}, f32[1,16]{1,0:T(1,128)S(1)}, u32[]{:S(2)}) copy-start(f32[1,16]{1,0:T(1,128)S(1)} %get-tuple-element.26) | copy-start | bytes 196
  50.9 32.5 %copy-start.35 = (f32[16]{0:T(128)}, f32[16]{0:T(128)S(1)}, u32[]{:S(2)}) copy-start(f32[16]{0:T(128)S(1)} %get-tuple-element.180) | copy-start | bytes 196
  50.9 32.6 %copy-start.29 = (f32[16]{0:T(128)}, f32[16]{0:T(128)S(1)}, u32[]{:S(2)}) copy-start(f32[16]{0:T(128)S(1)} %get-tuple-element.183) | copy-start | bytes 196
  50.9 32.7 %copy-start.27 = (f32[16]{0:T(128)}, f32[16]{0:T(128)S(1)}, u32[]{:S(2)}) copy-start(f32[16]{0:T(128)S(1)} %get-tuple-element.182) | copy-start | bytes 196
  50.9 32.9 %copy-start.25 = (f32[16]{0:T(128)}, f32[16]{0:T(128)S(1)}, u32[]{:S(2)}) copy-start(f32[16]{0:T(128)S(1)} %get-tuple-element.181) | copy-start | bytes 196
  50.9 454.7 %copy-start.21 = (f32[16]{0:T(128)}, f32[16]{0:T(128)S(1)}, u32[]{:S(2)}) copy-start(f32[16]{0:T(128)S(1)} %get-tuple-element.185) | copy-start | bytes 196
  50.9 455.6 %copy-start.24 = (f32[16]{0:T(128)}, f32[16]{0:T(128)S(1)}, u32[]{:S(2)}) copy-start(f32[16]{0:T(128)S(1)} %get-tuple-element.184) | copy-start | bytes 196
  54.6 26.5 %copy-start.43 = (f32[128]{0:T(128)}, f32[128]{0:T(128)S(1)}, u32[]{:S(2)}) copy-start(f32[128]{0:T(128)S(1)} %iota_convert_fusion) | copy-start | bytes 1540
  54.6 58.1 %copy-start.37 = (f32[16]{0:T(128)}, f32[16]{0:T(128)S(1)}, u32[]{:S(2)}) copy-start(f32[16]{0:T(128)S(1)} %get-tuple-element.171) | copy-start | bytes 196
  54.6 441.0 %copy-start.22 = (f32[16]{0:T(128)}, f32[16]{0:T(128)S(1)}, u32[]{:S(2)}) copy-start(f32[16]{0:T(128)S(1)} %get-tuple-element.172) | copy-start | bytes 196
  56.8 24.4 %copy-start.39 = (f32[128]{0:T(128)}, f32[128]{0:T(128)S(1)}, u32[]{:S(2)}) copy-start(f32[128]{0:T(128)S(1)} %broadcast_subtract_fusion) | copy-start | bytes 1540
  56.8 55.9 %copy-start.33 = (f32[128]{0:T(128)}, f32[128]{0:T(128)S(1)}, u32[]{:S(2)}) copy-start(f32[128]{0:T(128)S(1)} %broadcast_add_fusion) | copy-start | bytes 1540
  57.0 53.9 %copy-start.13 = (f32[128,16,1,1]{1,3,2,0:T(1,128)}, f32[128,16,1,1]{1,3,2,0:T(1,128)S(1)}, u32[]{:S(2)}) copy-start(f32[128,16,1,1]{1,3,2,0:T(1,128)S(1)} %pad_multiply_fusion) | copy-start | bytes 24580
  81.2 33.5 %copy-start.3 = (bf16[1,128,4096]{1,2,0:T(8,128)(2,1)}, bf16[1,128,4096]{1,2,0:T(8,128)(2,1)S(1)}, u32[]{:S(2)}) copy-start(bf16[1,128,4096]{1,2,0:T(8,128)(2,1)S(1)} %copy.779) | copy-start | bytes 3145732
  110.9 1.0 copy-start.7
  112.3 2.4 copy-start.15
  198.1 58.6 %all-to-all-start.3 = ((f32[128,1,128,32]{2,3,1,0:T(8,128)}), f32[128,1,128,32]{2,3,1,0:T(8,128)S(1)}, u32[]{:S(2)}, u32[]{:S(2)}) async-start(f32[128,1,128,32]{2,3,1,0:T(8,128)} %constant_dynamic-update-slice_fusion), calls=%async_computation.3 | async-start | bytes 4194304 | tf_op jit(solution)/shard_map/all_to_all | solution.py:134
  206.4 53.6 %copy-start.18 = (f32[128,128]{1,0:T(8,128)S(1)}, f32[128,128]{1,0:T(8,128)}, u32[]{:S(2)}) copy-start(f32[128,128]{1,0:T(8,128)} %param.13) | copy-start | bytes 196612
  258.0 87.4 %collective-permute-start.1 = (bf16[128,4096]{0,1:T(8,128)(2,1)}, bf16[128,4096]{0,1:T(8,128)(2,1)}, u32[]{:S(2)}, u32[]{:S(2)}) collective-permute-start(bf16[128,4096]{0,1:T(8,128)(2,1)} %fusion.7), channel_id=1, source_target_pairs={{0,1},{1,2},{2,3},{3,4},{4,5},{5,6},{6,7},{7,8},{8,9},{9,10},{10,1... | collective-permute-start | bytes 3145736 | tf_op jit(solution)/shard_map/ppermute | solution.py:11
  347.4 21.5 %copy-start.1 = (f32[128,4096]{0,1:T(8,128)}, f32[128,4096]{0,1:T(8,128)S(1)}, u32[]{:S(2)}) copy-start(f32[128,4096]{0,1:T(8,128)S(1)} %get-tuple-element.27) | copy-start | bytes 6291460
  347.4 21.5 %copy-start.2 = (f32[128,4096]{0,1:T(8,128)}, f32[128,4096]{0,1:T(8,128)S(1)}, u32[]{:S(2)}) copy-start(f32[128,4096]{0,1:T(8,128)S(1)} %get-tuple-element.28) | copy-start | bytes 6291460
  347.4 21.5 %copy-start.10 = (bf16[1,128,4096]{1,2,0:T(8,128)(2,1)S(1)}, bf16[1,128,4096]{1,2,0:T(8,128)(2,1)}, u32[]{:S(2)}) copy-start(bf16[1,128,4096]{1,2,0:T(8,128)(2,1)} %copy.623) | copy-start | bytes 3145732
  347.5 21.5 %copy-start.11 = (bf16[1,128,4096]{1,2,0:T(8,128)(2,1)S(1)}, bf16[1,128,4096]{1,2,0:T(8,128)(2,1)}, u32[]{:S(2)}) copy-start(bf16[1,128,4096]{1,2,0:T(8,128)(2,1)} %copy.624) | copy-start | bytes 3145732
  370.4 16.1 %copy-start.5 = (bf16[1,128,4096]{1,2,0:T(8,128)(2,1)}, bf16[1,128,4096]{1,2,0:T(8,128)(2,1)S(1)}, u32[]{:S(2)}) copy-start(bf16[1,128,4096]{1,2,0:T(8,128)(2,1)S(1)} %get-tuple-element.162) | copy-start | bytes 3145732
  370.4 16.1 %collective-permute-start = (bf16[128,4096]{0,1:T(8,128)(2,1)S(1)}, bf16[128,4096]{0,1:T(8,128)(2,1)S(1)}, u32[]{:S(2)}, u32[]{:S(2)}) collective-permute-start(bf16[128,4096]{0,1:T(8,128)(2,1)S(1)} %bitcast.617), channel_id=1, source_target_pairs={{1,0},{2,1},{3,2},{4,3},{5,4},{6,5},{7,6},{8,7},{9,8},{10,9},{11,1... | collective-permute-start | bytes 3145736 | tf_op jit(solution)/shard_map/ppermute | solution.py:11
  493.3 2.3 copy-start.40
  505.4 1.2 copy-start.26
  505.5 1.2 copy-start.28
  505.5 1.3 copy-start.30
  505.5 1.4 copy-start.36
  506.7 0.9 copy-start.17
  534.3 28.9 %slice-start = ((f32[64,16,1,32]{3,1,0,2:T(8,128)}), f32[1,16,1,32]{3,1,0,2:T(8,128)S(1)}, s32[]{:S(2)}) async-start(f32[64,16,1,32]{3,1,0,2:T(8,128)} %copy-done.12), calls=%async_computation.5 | async-start | bytes 16384 | tf_op jit(solution)/shard_map/slice | solution.py:75
  536.1 38.5 %copy-start.20 = (f32[1,16]{1,0:T(1,128)S(1)}, f32[1,16]{1,0:T(1,128)}, u32[]{:S(2)}) copy-start(f32[1,16]{1,0:T(1,128)} %copy-done.19) | copy-start | bytes 196
  574.6 1.4 copy-start.8
  574.6 1.5 copy-start.9
  597.1 23.7 %copy-start.14 = (f32[128,16,1,1]{1,3,2,0:T(1,128)S(1)}, f32[128,16,1,1]{1,3,2,0:T(1,128)}, u32[]{:S(2)}) copy-start(f32[128,16,1,1]{1,3,2,0:T(1,128)} %copy-done.13) | copy-start | bytes 24580
  621.7 3.5 copy-start
  621.7 3.5 copy-start.16
  752.5 7.6 copy-start.6
  752.5 436.6 %all-to-all-start.1 = ((bf16[128,2,2048]{2,1,0:T(2,128)(2,1)}), bf16[128,2,2048]{2,1,0:T(2,128)(2,1)}, u32[]{:S(2)}, u32[]{:S(2)}) async-start(bf16[128,2,2048]{2,1,0:T(2,128)(2,1)} %reshape.685), calls=%async_computation.1 | async-start | bytes 2097152 | tf_op jit(solution)/shard_map/all_to_all | solution.py:173
  760.0 337.1 %all-reduce.53.cloned.1.call-start = ((), (), s32[]{:S(2)}) async-start(), calls=%async_computation.4 | async-start | bytes 131072 | tf_op jit(solution)/shard_map/psum | solution.py:178
  858.7 242.5 %copy-start.4 = (bf16[1,128,4096]{1,2,0:T(8,128)(2,1)S(1)}, bf16[1,128,4096]{1,2,0:T(8,128)(2,1)}, u32[]{:S(2)}) copy-start(bf16[1,128,4096]{1,2,0:T(8,128)(2,1)} %copy-done.3) | copy-start | bytes 3145732
  1103.1 10.6 copy-start.42
  1103.1 10.6 copy-start.44
  (4 other events, 3.4 us)
Sparse Core Ops, SparseCore 0:
  858.8 238.2 all-reduce.52
